TPU v7x, 256 devices: a whole 4x4x8 slice. The times are simulated.
256 devices in a mesh: row: 8 (over z), col: 16 (over y, x), rep: 2 (over core).
Axes of the slice: x: 4, y: 4, z: 8, core: 2. Of those that a mesh axis runs over, the one named last changes fastest.
Arguments:
- amplitudes: bfloat16 [4, 512, 16384], P(None, 'col', ('row', 'rep')), may hold values from -6 to 6
- ladder_integrals: bfloat16 [4, 16384, 16384], P(None, ('row', 'rep'), 'col'), may hold values from -0.046875 to 0.046875
- hole_integrals: bfloat16 [4, 512, 4, 512], P(None, ('row', 'rep'), None, 'col'), may hold values from -0.25 to 0.25
- denominators: float32 [4, 512, 16384], P(None, ('row', 'rep'), 'col'), may hold values from 1 to 10
- pair_irrep: int32 [4], replicated, may hold values from 0 to 7
- irrep_pairs: int32 [8], replicated, may hold values from 1 to 16384, 81920 in all
Outputs:
- update: bfloat16 [4, 512, 16384], P(None, ('row', 'rep'), 'col')
Inputs may be any that keep to these rules, and one draw needn't show every extreme that they name: `irrep_pairs`: one irrep product has 16384 used virtual pairs.
All inputs are finite; a program needn't handle non-finite values.
Results may differ from a plain program's by a relative error of at most 0.001.
Values may be sent and summed in bfloat16 or wider, within the bound.
A program may use at most 128 MiB of HBM per device.

v0:
```python
import jax
import jax.numpy as jnp
from jax import lax
from jax.sharding import PartitionSpec as P


def per_device(amplitudes, ladder_integrals, hole_integrals, denominators, pair_irrep, irrep_pairs):
    local_cols = amplitudes.shape[2]
    output_cols = denominators.shape[2]
    irreps = jnp.arange(irrep_pairs.shape[0], dtype=jnp.int32)
    limits = jnp.sum(
        jnp.where(pair_irrep[:, None] == irreps[None, :], irrep_pairs[None, :], 0), axis=1
    )
    row_start = lax.axis_index(("row", "rep")) * local_cols
    col_start = lax.axis_index("col") * output_cols
    inside = (row_start + jnp.arange(local_cols, dtype=jnp.int32))[None, :] < limits[:, None]
    masked = jnp.where(inside[:, None, :], amplitudes, jnp.zeros_like(amplitudes))
    alike = pair_irrep[:, None] == pair_irrep[None, :]
    weights = jnp.where(alike[:, None, :, None], hole_integrals, jnp.zeros_like(hole_integrals))
    gathered = lax.all_gather(masked, "col", axis=1, tiled=True)
    partial_value = jnp.einsum(
        "qpc,qca->qpa", gathered, ladder_integrals, preferred_element_type=jnp.float32
    )
    ladder_term = lax.psum_scatter(partial_value, ("row", "rep"), scatter_dimension=1, tiled=True)
    spread = lax.all_gather(masked, ("row", "rep"), axis=2, tiled=True)
    partial_value = jnp.einsum("qpsr,sra->qpa", weights, spread, preferred_element_type=jnp.float32)
    hole_term = lax.psum_scatter(partial_value, "col", scatter_dimension=2, tiled=True)
    kept_cols = (col_start + jnp.arange(output_cols, dtype=jnp.int32))[None, :] < limits[:, None]
    combined = (ladder_term + hole_term) / denominators
    return jnp.where(kept_cols[:, None, :], combined, jnp.float32(0.0)).astype(jnp.bfloat16)


def solution(mesh):
    return jax.shard_map(
        per_device,
        mesh=mesh,
        in_specs=(
            P(None, "col", ("row", "rep")),
            P(None, ("row", "rep"), "col"),
            P(None, ("row", "rep"), None, "col"),
            P(None, ("row", "rep"), "col"),
            P(),
            P(),
        ),
        out_specs=P(None, ("row", "rep"), "col"),
        check_vma=False,
    )
```

profile of v0, /device:TPU:4, one launch (start us, length us, event | category | flops | bytes accessed | tf_op | source)
XLA Modules:
  0.0 286.3 jit_solution(4876944140708041479)
XLA Ops:
  6.5 0.0 all-gather.5.cloned.1.call-start
  6.5 0.9 select_reduce_fusion
  7.4 0.1 broadcast_compare_fusion.1
  7.5 1.7 broadcast_select_fusion
  9.2 0.0 all-gather.5.cloned.1.call-update
  9.2 0.0 all-gather.3.cloned.1.call-start
  9.2 0.7 all-gather.3.cloned.1.call-update
  9.9 0.0 reduce-scatter.5.cloned.1.call-start
  10.0 0.8 broadcast_compare_fusion.2
  10.8 1.0 broadcast_select_fusion.1
  11.8 42.6 %all-gather.5.cloned.1.call-done = bf16[4,32,16384]{2,1,0:T(8,128)(2,1)} async-done(((bf16[4,32,1024]{2,1,0:T(8,128)(2,1)}), bf16[4,32,16384]{2,1,0:T(8,128)(2,1)}) %all-gather.5.cloned.1.call-update) | async-done | bytes 4194320 | tf_op jit(solution)/shard_map/all_gather | solution.py:25
  54.4 6.7 %convolution_bitcast_fusion = f32[4,32,16384]{2,1,0:T(8,128)} fusion(bf16[4,32,16384]{2,1,0:T(8,128)(2,1)} %all-gather.5.cloned.1.call-done, bf16[4,32,4,32]{3,2,1,0:T(4,128)(2,1)S(1)} %broadcast_select_fusion.1), kind=kOutput, calls=%fused_computation | convolution fusion | flops 536870912 | bytes 12615680 | tf_op jit(solution)/shard_map/qpsr,sra->qpa/dot_general | solution.py:26
  61.1 0.0 reduce-scatter.5.cloned.1.call-update
  61.1 0.0 reduce-scatter.3.cloned.1.call-start
  61.2 50.9 %all-gather.3.cloned.1.call-done = bf16[4,512,1024]{2,1,0:T(8,128)(2,1)} async-done(((bf16[4,32,1024]{2,1,0:T(8,128)(2,1)}), bf16[4,512,1024]{2,1,0:T(8,128)(2,1)}) %all-gather.3.cloned.1.call-update) | async-done | bytes 4194320 | tf_op jit(solution)/shard_map/all_gather | solution.py:20
  112.1 12.4 %fusion.2 = f32[4,512,1024]{2,1,0:T(8,128)} fusion(bf16[4,512,1024]{2,1,0:T(8,128)(2,1)} %all-gather.3.cloned.1.call-done, bf16[4,1024,1024]{2,1,0:T(8,128)(2,1)} %param.7), kind=kOutput, calls=%fused_computation.13 | convolution fusion | flops 4294967296 | bytes 20971520 | tf_op jit(solution)/shard_map/qpc,qca->qpa/dot_general | solution.py:21
  124.5 0.0 copy-start
  124.5 0.0 reduce-scatter.3.cloned.1.call-update
  124.5 80.4 %reduce-scatter.5.cloned.1.call-done = f32[4,32,1024]{2,1,0:T(8,128)} async-done(((f32[4,32,16384]{2,1,0:T(8,128)}), f32[4,32,1024]{2,1,0:T(8,128)}) %reduce-scatter.5.cloned.1.call-update) | async-done | bytes 524304 | tf_op jit(solution)/shard_map/reduce_scatter | solution.py:27
  204.9 72.8 %reduce-scatter.3.cloned.1.call-done = f32[4,32,1024]{2,1,0:T(8,128)} async-done(((f32[4,512,1024]{2,1,0:T(8,128)}), f32[4,32,1024]{2,1,0:T(8,128)}) %reduce-scatter.3.cloned.1.call-update) | async-done | bytes 524304 | tf_op jit(solution)/shard_map/reduce_scatter | solution.py:24
  277.7 0.0 copy-done
  277.7 2.1 select_convert_fusion
  (1 shorter events, 0.0 us)
Async XLA Ops:
  6.5 47.9 %all-gather.5.cloned.1.call-start = ((), (), s32[]{:S(2)}) async-start(), calls=%async_computation.4 | async-start | bytes 4456448 | tf_op jit(solution)/shard_map/all_gather | solution.py:25
  9.2 102.9 %all-gather.3.cloned.1.call-start = ((), (), s32[]{:S(2)}) async-start(), calls=%async_computation.2 | async-start | bytes 4456448 | tf_op jit(solution)/shard_map/all_gather | solution.py:20
  9.9 195.0 %reduce-scatter.5.cloned.1.call-start = ((), (), s32[]{:S(2)}) async-start(), calls=%async_computation.5 | async-start | bytes 8912896 | tf_op jit(solution)/shard_map/reduce_scatter | solution.py:27
  61.1 216.6 %reduce-scatter.3.cloned.1.call-start = ((), (), s32[]{:S(2)}) async-start(), calls=%async_computation.3 | async-start | bytes 8912896 | tf_op jit(solution)/shard_map/reduce_scatter | solution.py:24
  124.5 153.3 %copy-start = (f32[4,32,1024]{2,1,0:T(8,128)S(1)}, f32[4,32,1024]{2,1,0:T(8,128)}, u32[]{:S(2)}) copy-start(f32[4,32,1024]{2,1,0:T(8,128)} %param.9) | copy-start | bytes 1572868
Sparse Core Ops, SparseCore 0:
  9.3 45.0 all-gather.4
  56.8 55.1 all-gather.2
  115.8 89.1 reduce-scatter.4
  207.3 70.3 reduce-scatter.2
where the time goes:
time: 287 us; the launch traced here: 286 us
  waiting for transfers between devices  247 us (86%)
  matrix products  19.1 us (7%)
  between operations  13.1 us (5%)
  other arithmetic  6.52 us (2%)
    reduce_scatter x1, waiting for transfers between devices, per_device(): lax.psum_scatter(partial_value, 'col', scatter_dimension=2, tiled=True)  80.4 us
    reduce_scatter x1, waiting for transfers between devices, per_device(): lax.psum_scatter(partial_value, ('row', 'rep'), scatter_dimension=1, tile...  72.8 us
    all_gather x1, waiting for transfers between devices, per_device(): gathered = lax.all_gather(masked, 'col', axis=1, tiled=True)  50.9 us
    all_gather x1, waiting for transfers between devices, per_device(): spread = lax.all_gather(masked, ('row', 'rep'), axis=2, tiled=True)  42.6 us
    dot_general x1, matrix products, per_device(): jnp.einsum('qpc,qca->qpa', gathered, ladder_integrals, preferred_element_...  12.4 us
    dot_general x1, matrix products, per_device(): jnp.einsum('qpsr,sra->qpa', weights, spread, preferred_element_type=jnp.f...  6.71 us
  transfers between devices with their start and end apart: 4, of which 4 were waited for; matrix products, arithmetic and copies ran while one was open for 7% of the time, Pallas kernels for 0%

commit v1 on v0

v1 whole, which is shorter than its diff:
```python
import functools

import jax
import jax.numpy as jnp
from jax import lax
from jax.experimental import pallas as pl
from jax.experimental.pallas import tpu as pltpu
from jax.sharding import PartitionSpec as P

MESH = pl.DeviceIdType.MESH
NQ, NIRR, BLK, KC, NA = 4, 8, 32, 1024, 1024
HALF = BLK // 2
MSG = NA + 128


def plane_of(b_y, b_x):
    return 2 * ((b_x + b_y) % 4) + b_y % 2, b_y // 2


def block_of(z, k):
    b_y = 2 * k + z % 2
    return b_y, (z // 2 + 4 - b_y) % 4


def encode(value):
    top = jnp.max(jnp.abs(value), axis=1, keepdims=True)
    step = jnp.ceil(8.0 * jnp.log2(jnp.maximum(top, 1e-30) * (1.0 / 32760.0)))
    scaled = jnp.round(value * jnp.exp2(step * -0.125))
    scaled = jnp.minimum(jnp.maximum(scaled, -32767.0), 32767.0)
    step = jnp.broadcast_to(step, (value.shape[0], 128))
    return scaled.astype(jnp.int32).astype(jnp.int16), step.astype(jnp.int32).astype(jnp.int16)


def widen(coded):
    low = coded.astype(jnp.int32) & 0xFFFF
    return ((low ^ 0x8000) - 0x8000).astype(jnp.float32)


def decode(coded, step):
    return widen(coded) * jnp.exp2(widen(step)[:, :1] * 0.125)


def kernel(pair_ref, used_ref, amp, ints, hole, den, out,
           tvm, g, wg, bt, dvm, am, wm, p_out, p_own, p_in, sbuf, rbuf,
           loc_sem, p1s, p1r, p2s, p2r, w0s, w0r, w1s, w1r, w2s, w2r, ats, atr, cs, cr, zs, zr):
    z, c, k = lax.axis_index("row"), lax.axis_index("col"), lax.axis_index("rep")
    y, x = c // 4, c % 4
    xh, xk = x // 2, x % 2
    r = 2 * z + k

    def xmate(d):
        return (z, y * 4 + (x + d) % 4, k)

    def ymate(d):
        return (z, ((y + d) % 4) * 4 + x, k)

    my_bz, my_bk = plane_of(y, x)
    own_y, own_x = block_of(z, k)
    phi_r = (r // 4 + r % 4) % 4
    phi_c = (c // 4 + c % 4) % 4
    w_to = (my_bz, r, my_bk)
    w_from = (c // 2, 4 * own_y + own_x, c % 2)
    xb = (x + phi_r) % 4
    yb = (y + phi_r) % 4
    z0, k0 = plane_of(y, xb)
    z1, k1 = plane_of(yb, x)
    a_to = ((z0, r, k0), (z1, r, k1))
    a_from = (
        (c // 2, 4 * own_y + (own_x + 4 - phi_c) % 4, c % 2),
        (c // 2, 4 * ((own_y + 4 - phi_c) % 4) + own_x, c % 2),
    )

    def is_me(dev):
        return (dev[0] == z) & (dev[1] == c) & (dev[2] == k)

    loads = [pltpu.make_async_copy(amp, g.at[:, y, xh, xk], loc_sem.at[0])]
    loads += [pltpu.make_async_copy(ints.at[q], tvm.at[q], loc_sem.at[1 + q]) for q in range(NQ)]
    loads += [pltpu.make_async_copy(den, dvm, loc_sem.at[5])]
    for load in loads:
        load.start()

    bar = pltpu.get_barrier_semaphore()

    def greet(dev):
        pl.semaphore_signal(bar, inc=1, device_id=dev, device_id_type=MESH)

    for d in (1, 2, 3):
        greet(xmate(d))
        greet(ymate(d))
    greet((z, c, 1 - k))
    greet(((z + 1) % 8, c, k))
    greet(((z + 7) % 8, c, k))
    for to, source in ((w_to, w_from), (a_to[0], a_from[0]), (a_to[1], a_from[1])):
        greet(to)
        greet(source)

    pl.semaphore_wait(bar, 15)

    def remote(src, dst, ssem, rsem, dev):
        return pltpu.make_async_remote_copy(
            src_ref=src, dst_ref=dst, send_sem=ssem, recv_sem=rsem, device_id=dev, device_id_type=MESH)

    def moved(src, dst, ssem, rsem, to):
        far = remote(src, dst, ssem, rsem, to)
        near = pltpu.make_async_copy(src, dst, rsem)

        def start():
            pl.when(is_me(to))(near.start)
            pl.when(jnp.logical_not(is_me(to)))(far.start)

        def wait():
            pl.when(is_me(to))(near.wait)
            pl.when(jnp.logical_not(is_me(to)))(far.wait)

        return start, wait

    lo, hi = pl.ds(0, HALF), pl.ds(HALF, HALF)
    w_start, w_wait = moved(hole, wg.at[:, r // 4, (r % 4) // 2, r % 2], w0s, w0r, w_to)
    w_start()

    def first(q):
        cps = []
        for d in (1, 2, 3):
            cps.append(remote(amp.at[q, lo], g.at[q, y, xh, xk, lo], p1s.at[q, 0, d - 1], p1r.at[q, 0, d - 1], xmate(d)))
            cps.append(remote(amp.at[q, hi], g.at[q, y, xh, xk, hi], p1s.at[q, 1, d - 1], p1r.at[q, 1, d - 1], ymate(d)))
        return cps

    def second(q):
        cps = []
        for d in (1, 2, 3):
            row = g.at[q, y, :, :, lo]
            col = g.at[q, :, xh, xk, hi]
            cps.append(remote(row, row, p2s.at[q, 0, d - 1], p2r.at[q, 0, d - 1], ymate(d)))
            cps.append(remote(col, col, p2s.at[q, 1, d - 1], p2r.at[q, 1, d - 1], xmate(d)))
        return cps

    firsts = [first(q) for q in range(NQ)]
    seconds = [second(q) for q in range(NQ)]
    w_first, w_second = [], []
    for d in (1, 2, 3):
        own_lo, own_hi = wg.at[:, y, xh, xk, lo], wg.at[:, y, xh, xk, hi]
        row, col = wg.at[:, y, :, :, lo], wg.at[:, :, xh, xk, hi]
        w_first.append(remote(own_lo, own_lo, w1s.at[0, d - 1], w1r.at[0, d - 1], xmate(d)))
        w_first.append(remote(own_hi, own_hi, w1s.at[1, d - 1], w1r.at[1, d - 1], ymate(d)))
        w_second.append(remote(row, row, w2s.at[0, d - 1], w2r.at[0, d - 1], ymate(d)))
        w_second.append(remote(col, col, w2s.at[1, d - 1], w2r.at[1, d - 1], xmate(d)))

    for q in range(NQ):
        for cp in firsts[q]:
            cp.start()
    loads[0].wait()

    def finish_first(q):
        for cp in firsts[q]:
            cp.wait()
        for cp in seconds[q]:
            cp.start()

    finish_first(0)
    w_wait()
    for cp in w_first:
        cp.start()
    for q in range(1, NQ):
        finish_first(q)

    at0 = moved(g.at[:, y, xb // 2, xb % 2, lo], bt.at[:, lo], ats.at[0], atr.at[0], a_to[0])
    at1 = moved(g.at[:, yb, xh, xk, hi], bt.at[:, hi], ats.at[1], atr.at[1], a_to[1])
    at0[0]()
    at1[0]()
    for cp in w_first:
        cp.wait()
    for cp in w_second:
        cp.start()

    limits = []
    for q in range(NQ):
        limit = 0
        for i in range(NIRR):
            limit = limit + jnp.where(pair_ref[q] == i, used_ref[i], 0)
        limits.append(limit)
    lane = lax.broadcasted_iota(jnp.int32, (HALF, KC), 1)
    lane_w = lax.broadcasted_iota(jnp.int32, (HALF, 128), 1) // BLK
    out_lane = lax.broadcasted_iota(jnp.int32, (BLK, NA), 1)

    def keep(rows, mask):
        tiles = rows.reshape(-1, HALF, rows.shape[-1]) * mask[None]
        return tiles.reshape(rows.shape)

    for cp in w_second:
        cp.wait()
    at0[1]()
    at1[1]()
    for q in range(NQ):
        inside = jnp.where(c * NA + lane < limits[q], 1.0, 0.0).astype(jnp.bfloat16)
        bt[q] = keep(bt[q], inside)

    def product(q, side, dst):
        inside = jnp.where(r * KC + lane < limits[q], 1.0, 0.0).astype(jnp.bfloat16)
        am[...] = keep(g[q, :, :, side].reshape(8 * BLK, KC), inside)
        alike = jnp.zeros((HALF, 128), jnp.float32)
        for q2 in range(NQ):
            same = jnp.where(pair_ref[q] == pair_ref[q2], 1.0, 0.0)
            alike = jnp.where(lane_w == q2, same, alike)
        wm[...] = keep(wg[q, :, :, side].reshape(8 * BLK, 128), alike.astype(jnp.bfloat16))

        @pl.loop(0, NA // 256)
        def _(n):
            cols = pl.ds(pl.multiple_of(n * 256, 256), 256)
            total = jnp.dot(am[...], tvm[q, :, cols], preferred_element_type=jnp.float32)
            held = bt[:, :, cols].reshape(NQ * BLK, 256)
            total += jnp.dot(wm[...], held, preferred_element_type=jnp.float32)
            dst[q, :, :, cols] = total.reshape(8, BLK, 256)

    swaps = [remote(p_out.at[q], p_in.at[q], cs.at[q], cr.at[q], (z, c, 1 - k)) for q in range(NQ)]

    def compute(q):
        loads[1 + q].wait()
        for cp in seconds[q]:
            cp.wait()
        product(q, 1 - k, p_out)
        swaps[q].start()
        product(q, k, p_own)

    def hops(q, way):
        return 4 if (q + way) % 2 == 0 else 3

    def link(q, way, h):
        i = way * 4 + h
        to = (z + 1) % 8 if way == 0 else (z + 7) % 8
        return remote(sbuf.at[q, i], rbuf.at[q, i], zs.at[q, i], zr.at[q, i], (to, c, k))

    def received(q, way, h):
        i = way * 4 + h
        link(q, way, h).wait_recv()
        return decode(rbuf[q, i, :, :NA], rbuf[q, i, :, NA:])

    def hop(q, h):
        for way in (0, 1):
            n = hops(q, way)
            if h >= n:
                continue
            far = n - h
            owner = (z + far) % 8 if way == 0 else (z + 8 - far) % 8
            total = p_own[q, owner] + p_in[q, owner]
            if h > 0:
                total += received(q, way, h - 1)
            coded, step = encode(total)
            i = way * 4 + h
            sbuf[q, i, :, :NA] = coded
            sbuf[q, i, :, NA:] = step
            link(q, way, h).start()

    def final(q):
        total = p_own[q, z] + p_in[q, z]
        total += received(q, 0, hops(q, 0) - 1)
        total += received(q, 1, hops(q, 1) - 1)
        total = total / dvm[q]
        out[q] = jnp.where(c * NA + out_lane < limits[q], total, 0.0).astype(jnp.bfloat16)

    for s in range(NQ + 5):
        t = s - 1
        if 0 <= t < NQ:
            swaps[t].wait()
            hop(t, 0)
        if s == 1:
            loads[5].wait()
        for h in (1, 2, 3):
            t = s - 1 - h
            if 0 <= t < NQ:
                hop(t, h)
        t = s - 5
        if 0 <= t < NQ:
            final(t)
        if s < NQ:
            compute(s)

    for q in range(NQ):
        for way in (0, 1):
            for h in range(hops(q, way)):
                link(q, way, h).wait_send()


def per_device(amplitudes, ladder_integrals, hole_integrals, denominators, pair_irrep, irrep_pairs):
    hole = hole_integrals.reshape(NQ, BLK, NQ * BLK)
    anywhere = pl.BlockSpec(memory_space=pl.ANY)
    smem = pl.BlockSpec(memory_space=pltpu.SMEM)
    bf16, f32 = jnp.bfloat16, jnp.float32
    dma = pltpu.SemaphoreType.DMA
    return pl.pallas_call(
        kernel,
        out_shape=jax.ShapeDtypeStruct((NQ, BLK, NA), bf16),
        in_specs=[smem, smem, anywhere, anywhere, anywhere, anywhere],
        out_specs=pl.BlockSpec(memory_space=pltpu.VMEM),
        scratch_shapes=[
            pltpu.VMEM((NQ, KC, NA), bf16),
            pltpu.VMEM((NQ, 4, 2, 2, BLK, KC), bf16),
            pltpu.VMEM((NQ, 4, 2, 2, BLK, 128), bf16),
            pltpu.VMEM((NQ, BLK, NA), bf16),
            pltpu.VMEM((NQ, BLK, NA), f32),
            pltpu.VMEM((8 * BLK, KC), bf16),
            pltpu.VMEM((8 * BLK, 128), bf16),
            pltpu.VMEM((NQ, 8, BLK, NA), f32),
            pltpu.VMEM((NQ, 8, BLK, NA), f32),
            pltpu.VMEM((NQ, 8, BLK, NA), f32),
            pltpu.VMEM((NQ, 8, BLK, MSG), jnp.int16),
            pltpu.VMEM((NQ, 8, BLK, MSG), jnp.int16),
            dma((6,)),
            dma((NQ, 2, 3)), dma((NQ, 2, 3)), dma((NQ, 2, 3)), dma((NQ, 2, 3)),
            dma, dma,
            dma((2, 3)), dma((2, 3)), dma((2, 3)), dma((2, 3)),
            dma((2,)), dma((2,)),
            dma((NQ,)), dma((NQ,)),
            dma((NQ, 8)), dma((NQ, 8)),
        ],
        compiler_params=pltpu.CompilerParams(
            collective_id=0, has_side_effects=True, vmem_limit_bytes=52 * 1024 * 1024),
    )(pair_irrep, irrep_pairs, amplitudes, ladder_integrals, hole, denominators)


def solution(mesh):
    return jax.shard_map(
        per_device,
        mesh=mesh,
        in_specs=(
            P(None, "col", ("row", "rep")),
            P(None, ("row", "rep"), "col"),
            P(None, ("row", "rep"), None, "col"),
            P(None, ("row", "rep"), "col"),
            P(),
            P(),
        ),
        out_specs=P(None, ("row", "rep"), "col"),
        check_vma=False,
    )
```

time: 287 us -> 94.8 us (0.33)
  the two profiles are of different devices: /device:TPU:4 before, /device:TPU:64 now
where the time goes in v1:
time: 94.8 us; the launch traced here: 94.7 us
  Pallas kernels  89.6 us (95%)
  local copies, waits for them, and re-layouts  5.04 us (5%)
    pallas_call x1, Pallas kernels, per_device(): pl.pallas_call(kernel, out_shape=jax.ShapeDtypeStruct((NQ, BLK, NA), bf16...  89.6 us
    unnamed x9, local copies, waits for them, and re-layouts  4 us

profile of v1, /device:TPU:64, one launch (start us, length us, event | category | flops | bytes accessed | tf_op | source)
XLA Modules:
  0.0 94.7 jit_solution(12956116910489991988)
XLA Ops:
  0.0 1.0 %reshape.3.hole = bf16[4,32,128]{2,1,0:T(8,128)(2,1)S(1)} reshape(bf16[4,32,4,32]{3,2,1,0:T(4,128)(2,1)} %param.8) | data formatting | bytes 65536 | tf_op jit(solution)/shard_map/reshape | solution.py:284
  1.0 0.0 copy-start
  1.1 1.0 %copy-done = f32[4,32,1024]{2,1,0:T(8,128)S(1)} copy-done((f32[4,32,1024]{2,1,0:T(8,128)S(1)}, f32[4,32,1024]{2,1,0:T(8,128)}, u32[]{:S(2)}) %copy-start) | copy-done | bytes 524312
  2.1 0.0 copy-start.1
  2.1 0.9 %copy-done.1 = bf16[4,32,1024]{2,1,0:T(8,128)(2,1)S(1)} copy-done((bf16[4,32,1024]{2,1,0:T(8,128)(2,1)S(1)}, bf16[4,32,1024]{2,1,0:T(8,128)(2,1)}, u32[]{:S(2)}) %copy-start.1) | copy-done | bytes 262168
  3.0 0.0 copy-start.2
  3.0 0.7 copy-done.2
  3.7 0.0 copy-start.3
  3.7 0.7 copy-done.3
  4.4 89.6 %shard_map.64 = bf16[4,32,1024]{2,1,0:T(8,128)(2,1)S(1)} custom-call(s32[4]{0:T(128)S(1)} %copy-done.2, s32[8]{0:T(128)S(1)} %copy-done.3, bf16[4,32,1024]{2,1,0:T(8,128)(2,1)S(1)} %copy-done.1, bf16[4,1024,1024]{2,1,0:T(8,128)(2,1)} %ints.1, bf16[4,32,128]{2,1,0:T(8,128)(2,1)S(1)} %reshape.3.hole, f32[4,32,1024]{2,1,0:T(8,128)S(1)} %copy-done), custom_call_target="tpu_custom_call" | custom-call | tf_op jit(solution)/shard_map/pallas_call | solution.py:289
  94.0 0.7 copy.8
Async XLA Ops:
  1.0 1.0 %copy-start = (f32[4,32,1024]{2,1,0:T(8,128)S(1)}, f32[4,32,1024]{2,1,0:T(8,128)}, u32[]{:S(2)}) copy-start(f32[4,32,1024]{2,1,0:T(8,128)} %den.1) | copy-start | bytes 1572868
  2.1 0.9 %copy-start.1 = (bf16[4,32,1024]{2,1,0:T(8,128)(2,1)S(1)}, bf16[4,32,1024]{2,1,0:T(8,128)(2,1)}, u32[]{:S(2)}) copy-start(bf16[4,32,1024]{2,1,0:T(8,128)(2,1)} %amp.1) | copy-start | bytes 786436
  3.0 0.7 copy-start.2
  3.7 0.7 copy-start.3

commit v2 on v1

v2 whole, which is shorter than its diff:
```python
import functools

import jax
import jax.numpy as jnp
from jax import lax
from jax.experimental import pallas as pl
from jax.experimental.pallas import tpu as pltpu
from jax.sharding import PartitionSpec as P

MESH = pl.DeviceIdType.MESH
NQ, NIRR, BLK, KC, NA = 4, 8, 32, 1024, 1024
HALF = BLK // 2
MSG = NA + 128
CHUNKS = [(q, pl.ds(0, BLK)) for q in range(NQ - 1)] + [(NQ - 1, pl.ds(0, HALF)), (NQ - 1, pl.ds(HALF, HALF))]
NT = len(CHUNKS)
CHAINED = 2
WIDE = 512


def plane_of(b_y, b_x):
    return 2 * ((b_x + b_y) % 4) + b_y % 2, b_y // 2


def block_of(z, k):
    b_y = 2 * k + z % 2
    return b_y, (z // 2 + 4 - b_y) % 4


def encode(value):
    top = jnp.max(jnp.abs(value), axis=1, keepdims=True)
    step = jnp.ceil(8.0 * jnp.log2(jnp.maximum(top, 1e-30) * (1.0 / 32760.0)))
    scaled = jnp.round(value * jnp.exp2(step * -0.125))
    scaled = jnp.minimum(jnp.maximum(scaled, -32767.0), 32767.0)
    step = jnp.broadcast_to(step, (value.shape[0], 128))
    return scaled.astype(jnp.int32).astype(jnp.int16), step.astype(jnp.int32).astype(jnp.int16)


def widen(coded):
    low = coded.astype(jnp.int32) & 0xFFFF
    return ((low ^ 0x8000) - 0x8000).astype(jnp.float32)


def decode(coded, step):
    return widen(coded) * jnp.exp2(widen(step)[:, :1] * 0.125)


def kernel(pair_ref, used_ref, amp, ints, hole, den, out,
           tvm, g, wg, bt, dvm, am, wm, p_out, p_own, p_in, sbuf, rbuf,
           loc_sem, p1s, p1r, p2s, p2r, p3s, p3r, w0s, w0r, w1s, w1r, w2s, w2r, as_, ar, cs, cr, zs, zr):
    z, c, k = lax.axis_index("row"), lax.axis_index("col"), lax.axis_index("rep")
    y, x = c // 4, c % 4
    xh, xk = x // 2, x % 2
    r = 2 * z + k

    def xmate(d):
        return (z, y * 4 + (x + d) % 4, k)

    def ymate(d):
        return (z, ((y + d) % 4) * 4 + x, k)

    my_bz, my_bk = plane_of(y, x)
    own_y, own_x = block_of(z, k)
    phi_r = (r // 4 + r % 4) % 4
    phi_c = (c // 4 + c % 4) % 4
    w_to = (my_bz, r, my_bk)
    w_from = (c // 2, 4 * own_y + own_x, c % 2)
    xb = (x + phi_r) % 4
    yb = (y + phi_r) % 4
    z0, k0 = plane_of(y, xb)
    z1, k1 = plane_of(yb, x)
    a_to = ((z0, r, k0), (z1, r, k1))
    a_from = (
        (c // 2, 4 * own_y + (own_x + 4 - phi_c) % 4, c % 2),
        (c // 2, 4 * ((own_y + 4 - phi_c) % 4) + own_x, c % 2),
    )

    def is_me(dev):
        return (dev[0] == z) & (dev[1] == c) & (dev[2] == k)

    loads = [pltpu.make_async_copy(amp, g.at[:, y, xh, xk], loc_sem.at[0])]
    loads += [pltpu.make_async_copy(ints.at[q], tvm.at[q], loc_sem.at[1 + q]) for q in range(NQ)]
    loads += [pltpu.make_async_copy(den, dvm, loc_sem.at[5])]
    for load in loads:
        load.start()

    bar = pltpu.get_barrier_semaphore()

    def greet(dev):
        pl.semaphore_signal(bar, inc=1, device_id=dev, device_id_type=MESH)

    for d in (1, 2, 3):
        greet(xmate(d))
        greet(ymate(d))
    greet((z, c, 1 - k))
    for d in (1, 2, 6, 7):
        greet(((z + d) % 8, c, k))
    for to, source in ((w_to, w_from), (a_to[0], a_from[0]), (a_to[1], a_from[1])):
        greet(to)
        greet(source)

    pl.semaphore_wait(bar, 17)

    def remote(src, dst, ssem, rsem, dev):
        return pltpu.make_async_remote_copy(
            src_ref=src, dst_ref=dst, send_sem=ssem, recv_sem=rsem, device_id=dev, device_id_type=MESH)

    def moved(src, dst, ssem, rsem, to):
        far = remote(src, dst, ssem, rsem, to)
        near = pltpu.make_async_copy(src, dst, rsem)

        def start():
            pl.when(is_me(to))(near.start)
            pl.when(jnp.logical_not(is_me(to)))(far.start)

        def wait():
            pl.when(is_me(to))(near.wait)
            pl.when(jnp.logical_not(is_me(to)))(far.wait)

        return start, wait

    lo, hi = pl.ds(0, HALF), pl.ds(HALF, HALF)
    w_start, w_wait = moved(hole, wg.at[:, r // 4, (r % 4) // 2, r % 2], w0s, w0r, w_to)
    w_start()

    left, right = pl.ds(0, KC // 2), pl.ds(KC // 2, KC // 2)
    y_up, y_dn, x_up, x_dn = (y + 1) % 4, (y + 3) % 4, (x + 1) % 4, (x + 3) % 4

    def first(q):
        cps = []
        for d in (1, 2, 3):
            cps.append(remote(amp.at[q, :, left], g.at[q, y, xh, xk, :, left], p1s.at[q, 0, d - 1], p1r.at[q, 0, d - 1], xmate(d)))
            cps.append(remote(amp.at[q, :, right], g.at[q, y, xh, xk, :, right], p1s.at[q, 1, d - 1], p1r.at[q, 1, d - 1], ymate(d)))
        return cps

    def second(t):
        q, rows = CHUNKS[t]
        row = g.at[q, y, :, :, rows, left]
        col = g.at[q, :, xh, xk, rows, right]
        cps = []
        for i, d in enumerate((1, 3)):
            cps.append(remote(row, row, p2s.at[t, 0, i], p2r.at[t, 0, i], ymate(d)))
            cps.append(remote(col, col, p2s.at[t, 1, i], p2r.at[t, 1, i], xmate(d)))
        return cps

    def third(t):
        q, rows = CHUNKS[t]
        pieces = (
            (g.at[q, y_dn, 0, :, rows, left], ymate(1)),
            (g.at[q, y_up, 1, :, rows, left], ymate(3)),
            (g.at[q, pl.ds(0, 2), x_dn // 2, x_dn % 2, rows, right], xmate(1)),
            (g.at[q, pl.ds(2, 2), x_up // 2, x_up % 2, rows, right], xmate(3)),
        )
        return [remote(ref, ref, p3s.at[t, i], p3r.at[t, i], to) for i, (ref, to) in enumerate(pieces)]

    firsts = [first(q) for q in range(NQ)]
    seconds = [second(t) for t in range(NT)]
    thirds = [third(t) for t in range(NT)]
    w_first, w_second = [], []
    for d in (1, 2, 3):
        own_lo, own_hi = wg.at[:, y, xh, xk, lo], wg.at[:, y, xh, xk, hi]
        row, col = wg.at[:, y, :, :, lo], wg.at[:, :, xh, xk, hi]
        w_first.append(remote(own_lo, own_lo, w1s.at[0, d - 1], w1r.at[0, d - 1], xmate(d)))
        w_first.append(remote(own_hi, own_hi, w1s.at[1, d - 1], w1r.at[1, d - 1], ymate(d)))
        w_second.append(remote(row, row, w2s.at[0, d - 1], w2r.at[0, d - 1], ymate(d)))
        w_second.append(remote(col, col, w2s.at[1, d - 1], w2r.at[1, d - 1], xmate(d)))

    def start(cps):
        for cp in cps:
            cp.start()

    def wait(cps):
        for cp in cps:
            cp.wait()

    ats = [
        (
            moved(g.at[q, y, xb // 2, xb % 2, :, left], bt.at[q, :, left], as_.at[q, 0], ar.at[q, 0], a_to[0]),
            moved(g.at[q, yb, xh, xk, :, right], bt.at[q, :, right], as_.at[q, 1], ar.at[q, 1], a_to[1]),
        )
        for q in range(NQ)
    ]

    def at_start(q):
        for go, _ in ats[q]:
            go()

    def at_wait(q):
        for _, hold in ats[q]:
            hold()

    for q in range(NQ):
        start(firsts[q])
    loads[0].wait()

    limits = []
    for q in range(NQ):
        limit = 0
        for i in range(NIRR):
            limit = limit + jnp.where(pair_ref[q] == i, used_ref[i], 0)
        limits.append(limit)
    lane = lax.broadcasted_iota(jnp.int32, (HALF, KC), 1)
    lane_w = lax.broadcasted_iota(jnp.int32, (HALF, 128), 1) // BLK

    def keep(rows, mask):
        tiles = rows.reshape(-1, HALF, rows.shape[-1]) * mask[None]
        return tiles.reshape(rows.shape)

    def mask_bt(q):
        inside = jnp.where(c * NA + lane < limits[q], 1.0, 0.0).astype(jnp.bfloat16)
        bt[q] = keep(bt[q], inside)

    def ladder(t, side, dst):
        q, rows = CHUNKS[t]
        m = 8 * rows.size
        inside = jnp.where(r * KC + lane < limits[q], 1.0, 0.0).astype(jnp.bfloat16)
        am[:m] = keep(g[q, :, :, side, rows].reshape(m, KC), inside)

        @pl.loop(0, NA // WIDE)
        def _(n):
            cols = pl.ds(pl.multiple_of(n * WIDE, WIDE), WIDE)
            total = jnp.dot(am[:m], tvm[q, :, cols], preferred_element_type=jnp.float32)
            dst[q, :, rows, cols] = total.reshape(8, rows.size, WIDE)

    def add_hole(t, side, dst):
        q, rows = CHUNKS[t]
        m = 8 * rows.size
        alike = jnp.zeros((HALF, 128), jnp.float32)
        for q2 in range(NQ):
            same = jnp.where(pair_ref[q] == pair_ref[q2], 1.0, 0.0)
            alike = jnp.where(lane_w == q2, same, alike)
        wm[:m] = keep(wg[q, :, :, side, rows].reshape(m, 128), alike.astype(jnp.bfloat16))

        @pl.loop(0, NA // WIDE)
        def _(n):
            cols = pl.ds(pl.multiple_of(n * WIDE, WIDE), WIDE)
            held = bt[:, :, cols].reshape(NQ * BLK, WIDE)
            total = jnp.dot(wm[:m], held, preferred_element_type=jnp.float32)
            dst[q, :, rows, cols] += total.reshape(8, rows.size, WIDE)

    swaps = []
    for t, (q, rows) in enumerate(CHUNKS):
        swaps.append(remote(p_out.at[q, :, rows], p_in.at[q, :, rows], cs.at[t], cr.at[t], (z, c, 1 - k)))

    def outer(t):
        ladder(t, 1 - k, p_out)
        add_hole(t, 1 - k, p_out)
        swaps[t].start()

    def inner(t):
        ladder(t, k, p_own)
        add_hole(t, k, p_own)

    def partial(t, owner):
        q, rows = CHUNKS[t]
        return p_own[q, owner, rows] + p_in[q, owner, rows]

    def post(t, i, total):
        n = CHUNKS[t][1].size
        coded, step = encode(total)
        sbuf[t, i, :n, :NA] = coded
        sbuf[t, i, :n, NA:] = step

    def letter(t, i, to):
        n = CHUNKS[t][1].size
        return remote(sbuf.at[t, i, :n], rbuf.at[t, i, :n], zs.at[t, i], zr.at[t, i], (to, c, k))

    def read(t, i):
        n = CHUNKS[t][1].size
        letter(t, i, (z + 1) % 8).wait_recv()
        return decode(rbuf[t, i, :n, :NA], rbuf[t, i, :n, NA:])

    def send_along(t, i, d, total):
        post(t, i, total)
        letter(t, i, (z + d + 8) % 8).start()

    def mine(t, d):
        return partial(t, (z + d + 8) % 8)

    def hops(t, way):
        return 4 if (t + way) % 2 == 0 else 3

    def chain(t, h):
        for way, d in ((0, 1), (1, -1)):
            n = hops(t, way)
            if h < n:
                total = mine(t, d * (n - h))
                if h > 0:
                    total += read(t, way * 4 + h - 1)
                send_along(t, way * 4 + h, d, total)

    def first_round(t):
        send_along(t, 4, -2 if t % 2 == 0 else 2, mine(t, 4))
        send_along(t, 1, 1, mine(t, 3))
        send_along(t, 2, -1, mine(t, -3))
        send_along(t, 0, 1, mine(t, -1))
        send_along(t, 3, -1, mine(t, 1))

    def second_round(t):
        down = mine(t, -2) + read(t, 0) + read(t, 2)
        up = mine(t, 2) + read(t, 1) + read(t, 3)
        if t % 2 == 0:
            send_along(t, 6, 2, up)
            send_along(t, 5, -2, down + read(t, 4))
        else:
            send_along(t, 5, -2, down)
            send_along(t, 6, 2, up + read(t, 4))

    def final(t):
        q, rows = CHUNKS[t]
        if t < CHAINED:
            total = mine(t, 0) + read(t, hops(t, 0) - 1) + read(t, 4 + hops(t, 1) - 1)
        else:
            total = mine(t, 0) + read(t, 5) + read(t, 6)
        total = total / dvm[q, rows]
        lanes = lax.broadcasted_iota(jnp.int32, (rows.size, NA), 1)
        out[q, rows] = jnp.where(c * NA + lanes < limits[q], total, 0.0).astype(jnp.bfloat16)

    def reduce(t):
        swaps[t].wait()
        if t < CHAINED:
            chain(t, 0)
        else:
            first_round(t)

    wait(firsts[0])
    start(seconds[0])
    at_start(0)
    for q in range(1, NQ):
        wait(firsts[q])
        at_start(q)
    w_wait()
    start(w_first)
    start(seconds[1])
    wait(seconds[0])
    start(thirds[0])
    wait(w_first)
    start(w_second)
    start(seconds[2])
    wait(seconds[1])
    start(thirds[1])
    start(seconds[3])
    start(seconds[4])
    for load in loads[1:]:
        load.wait()
    wait(thirds[0])
    ladder(0, 1 - k, p_out)
    ladder(0, k, p_own)
    wait(w_second)
    for q in range(NQ):
        at_wait(q)
        mask_bt(q)
    add_hole(0, 1 - k, p_out)
    swaps[0].start()
    add_hole(0, k, p_own)
    wait(seconds[2])
    start(thirds[2])
    wait(thirds[1])
    outer(1)
    reduce(0)
    inner(1)
    wait(seconds[3])
    start(thirds[3])
    wait(seconds[4])
    start(thirds[4])
    reduce(1)
    wait(thirds[2])
    outer(2)
    chain(0, 1)
    inner(2)
    wait(thirds[3])
    outer(3)
    reduce(2)
    chain(1, 1)
    inner(3)
    wait(thirds[4])
    outer(4)
    chain(0, 2)
    reduce(3)
    inner(4)
    reduce(4)
    chain(1, 2)
    second_round(2)
    chain(0, 3)
    second_round(3)
    chain(1, 3)
    second_round(4)
    final(0)
    final(2)
    final(3)
    final(1)
    final(4)

    for t in range(NT):
        used = range(7) if t >= CHAINED else [w * 4 + h for w in (0, 1) for h in range(hops(t, w))]
        for i in used:
            letter(t, i, (z + 1) % 8).wait_send()


def per_device(amplitudes, ladder_integrals, hole_integrals, denominators, pair_irrep, irrep_pairs):
    hole = hole_integrals.reshape(NQ, BLK, NQ * BLK)
    anywhere = pl.BlockSpec(memory_space=pl.ANY)
    smem = pl.BlockSpec(memory_space=pltpu.SMEM)
    bf16, f32 = jnp.bfloat16, jnp.float32
    dma = pltpu.SemaphoreType.DMA
    return pl.pallas_call(
        kernel,
        out_shape=jax.ShapeDtypeStruct((NQ, BLK, NA), bf16),
        in_specs=[smem, smem, anywhere, anywhere, anywhere, anywhere],
        out_specs=pl.BlockSpec(memory_space=pltpu.VMEM),
        scratch_shapes=[
            pltpu.VMEM((NQ, KC, NA), bf16),
            pltpu.VMEM((NQ, 4, 2, 2, BLK, KC), bf16),
            pltpu.VMEM((NQ, 4, 2, 2, BLK, 128), bf16),
            pltpu.VMEM((NQ, BLK, NA), bf16),
            pltpu.VMEM((NQ, BLK, NA), f32),
            pltpu.VMEM((8 * BLK, KC), bf16),
            pltpu.VMEM((8 * BLK, 128), bf16),
            pltpu.VMEM((NQ, 8, BLK, NA), f32),
            pltpu.VMEM((NQ, 8, BLK, NA), f32),
            pltpu.VMEM((NQ, 8, BLK, NA), f32),
            pltpu.VMEM((NT, 8, BLK, MSG), jnp.int16),
            pltpu.VMEM((NT, 8, BLK, MSG), jnp.int16),
            dma((6,)),
            dma((NQ, 2, 3)), dma((NQ, 2, 3)), dma((NT, 2, 2)), dma((NT, 2, 2)), dma((NT, 4)), dma((NT, 4)),
            dma, dma,
            dma((2, 3)), dma((2, 3)), dma((2, 3)), dma((2, 3)),
            dma((NQ, 2)), dma((NQ, 2)),
            dma((NT,)), dma((NT,)),
            dma((NT, 8)), dma((NT, 8)),
        ],
        compiler_params=pltpu.CompilerParams(
            collective_id=0, has_side_effects=True, vmem_limit_bytes=60 * 1024 * 1024),
    )(pair_irrep, irrep_pairs, amplitudes, ladder_integrals, hole, denominators)


def solution(mesh):
    return jax.shard_map(
        per_device,
        mesh=mesh,
        in_specs=(
            P(None, "col", ("row", "rep")),
            P(None, ("row", "rep"), "col"),
            P(None, ("row", "rep"), None, "col"),
            P(None, ("row", "rep"), "col"),
            P(),
            P(),
        ),
        out_specs=P(None, ("row", "rep"), "col"),
        check_vma=False,
    )
```

time: 94.8 us -> 81.5 us (0.86); the launches traced: 94.7 us -> 80.2 us
  Pallas kernels: 89.6 us -> 76.9 us
  local copies, waits for them, and re-layouts: 5.04 us -> 3.33 us
    pallas_call x1, Pallas kernels: 89.6 us -> 76.9 us  [per_device(): pl.pallas_call(kernel, out_shape=jax.ShapeDtypeStruct((NQ, BLK, NA), bf16...]
    unnamed x9 -> x1, local copies, waits for them, and re-layouts: 4 us -> 1.67 us
where the time goes in v2:
time: 81.5 us; the launch traced here: 80.2 us
  Pallas kernels  76.9 us (94%)
  local copies, waits for them, and re-layouts  3.33 us (4%)
    pallas_call x1, Pallas kernels, per_device(): pl.pallas_call(kernel, out_shape=jax.ShapeDtypeStruct((NQ, BLK, NA), bf16...  76.9 us
    unnamed x1, local copies, waits for them, and re-layouts  1.67 us
    reshape x1, local copies, waits for them, and re-layouts, per_device(): hole = hole_integrals.reshape(NQ, BLK, NQ * BLK)  1.66 us

profile of v2, /device:TPU:64, one launch (start us, length us, event | category | flops | bytes accessed | tf_op | source)
XLA Modules:
  0.0 80.2 jit_solution(7893480007448717434)
XLA Ops:
  0.0 1.7 %reshape.3.hole = bf16[4,32,128]{2,1,0:T(8,128)(2,1)} reshape(bf16[4,32,4,32]{3,2,1,0:T(4,128)(2,1)} %param.8) | data formatting | bytes 65536 | tf_op jit(solution)/shard_map/reshape | solution.py:400
  1.7 76.9 %shard_map.64 = bf16[4,32,1024]{2,1,0:T(8,128)(2,1)} custom-call(s32[4]{0:T(128)} %pair_ref.1, s32[8]{0:T(128)} %used_ref.1, bf16[4,32,1024]{2,1,0:T(8,128)(2,1)} %amp.1, bf16[4,1024,1024]{2,1,0:T(8,128)(2,1)} %ints.1, bf16[4,32,128]{2,1,0:T(8,128)(2,1)} %reshape.3.hole, f32[4,32,1024]{2,1,0:T(8,128)} %den.1), custom_call_target="tpu_custom_call" | custom-call | tf_op jit(solution)/shard_map/pallas_call | solution.py:405
  78.6 1.7 %copy.8 = bf16[4,32,1024]{2,1,0:T(8,128)(2,1)} copy(bf16[4,32,1024]{2,1,0:T(8,128)(2,1)} %shard_map.64) | data formatting | bytes 524288

commit v3 on v2

--- a/solution.py
+++ b/solution.py
@@ -13,8 +13,8 @@
 MSG = NA + 128
 CHUNKS = [(q, pl.ds(0, BLK)) for q in range(NQ - 1)] + [(NQ - 1, pl.ds(0, HALF)), (NQ - 1, pl.ds(HALF, HALF))]
 NT = len(CHUNKS)
-CHAINED = 2
-WIDE = 512
+CHAINED = 3
+WIDE = 1024
 
 
 def plane_of(b_y, b_x):
@@ -118,8 +118,7 @@
 
         return start, wait
 
-    lo, hi = pl.ds(0, HALF), pl.ds(HALF, HALF)
-    w_start, w_wait = moved(hole, wg.at[:, r // 4, (r % 4) // 2, r % 2], w0s, w0r, w_to)
+    w_start, w_wait = moved(hole, wg.at[r // 4, (r % 4) // 2, r % 2], w0s, w0r, w_to)
     w_start()
 
     left, right = pl.ds(0, KC // 2), pl.ds(KC // 2, KC // 2)
@@ -157,8 +156,8 @@
     thirds = [third(t) for t in range(NT)]
     w_first, w_second = [], []
     for d in (1, 2, 3):
-        own_lo, own_hi = wg.at[:, y, xh, xk, lo], wg.at[:, y, xh, xk, hi]
-        row, col = wg.at[:, y, :, :, lo], wg.at[:, :, xh, xk, hi]
+        own_lo, own_hi = wg.at[y, xh, xk, :2], wg.at[y, xh, xk, 2:]
+        row, col = wg.at[y, :, :, :2], wg.at[:, xh, xk, 2:]
         w_first.append(remote(own_lo, own_lo, w1s.at[0, d - 1], w1r.at[0, d - 1], xmate(d)))
         w_first.append(remote(own_hi, own_hi, w1s.at[1, d - 1], w1r.at[1, d - 1], ymate(d)))
         w_second.append(remote(row, row, w2s.at[0, d - 1], w2r.at[0, d - 1], ymate(d)))
@@ -228,7 +227,7 @@
         for q2 in range(NQ):
             same = jnp.where(pair_ref[q] == pair_ref[q2], 1.0, 0.0)
             alike = jnp.where(lane_w == q2, same, alike)
-        wm[:m] = keep(wg[q, :, :, side, rows].reshape(m, 128), alike.astype(jnp.bfloat16))
+        wm[:m] = keep(wg[:, :, side, q, rows].reshape(m, 128), alike.astype(jnp.bfloat16))
 
         @pl.loop(0, NA // WIDE)
         def _(n):
@@ -325,11 +324,11 @@
     wait(firsts[0])
     start(seconds[0])
     at_start(0)
+    w_wait()
+    start(w_first)
     for q in range(1, NQ):
         wait(firsts[q])
         at_start(q)
-    w_wait()
-    start(w_first)
     start(seconds[1])
     wait(seconds[0])
     start(thirds[0])
@@ -367,27 +366,29 @@
     outer(2)
     chain(0, 1)
     inner(2)
+    reduce(2)
+    chain(1, 1)
+    chain(0, 2)
     wait(thirds[3])
     outer(3)
-    reduce(2)
-    chain(1, 1)
     inner(3)
+    chain(2, 1)
+    chain(1, 2)
     wait(thirds[4])
     outer(4)
-    chain(0, 2)
     reduce(3)
+    chain(0, 3)
     inner(4)
     reduce(4)
-    chain(1, 2)
-    second_round(2)
-    chain(0, 3)
+    chain(2, 2)
+    chain(1, 3)
     second_round(3)
-    chain(1, 3)
+    final(0)
+    chain(2, 3)
     second_round(4)
-    final(0)
+    final(1)
+    final(3)
     final(2)
-    final(3)
-    final(1)
     final(4)
 
     for t in range(NT):
@@ -410,7 +411,7 @@
         scratch_shapes=[
             pltpu.VMEM((NQ, KC, NA), bf16),
             pltpu.VMEM((NQ, 4, 2, 2, BLK, KC), bf16),
-            pltpu.VMEM((NQ, 4, 2, 2, BLK, 128), bf16),
+            pltpu.VMEM((4, 2, 2, NQ, BLK, 128), bf16),
             pltpu.VMEM((NQ, BLK, NA), bf16),
             pltpu.VMEM((NQ, BLK, NA), f32),
             pltpu.VMEM((8 * BLK, KC), bf16),

time: 81.5 us -> 79.5 us (0.975)
  Pallas kernels: 76.9 us -> 74.7 us
    pallas_call x1, Pallas kernels: 76.9 us -> 74.7 us  [per_device(): pl.pallas_call(kernel, out_shape=jax.ShapeDtypeStruct((NQ, BLK, NA), bf16...]
where the time goes in v3:
time: 79.5 us; the launch traced here: 78.1 us
  Pallas kernels  74.7 us (94%)
  local copies, waits for them, and re-layouts  3.33 us (4%)
    pallas_call x1, Pallas kernels, per_device(): pl.pallas_call(kernel, out_shape=jax.ShapeDtypeStruct((NQ, BLK, NA), bf16...  74.7 us
    unnamed x1, local copies, waits for them, and re-layouts  1.67 us
    reshape x1, local copies, waits for them, and re-layouts, per_device(): hole = hole_integrals.reshape(NQ, BLK, NQ * BLK)  1.66 us

profile of v3, /device:TPU:64, one launch (start us, length us, event | category | flops | bytes accessed | tf_op | source)
XLA Modules:
  0.0 78.1 jit_solution(7941194924727866391)
XLA Ops:
  0.0 1.7 %reshape.3.hole = bf16[4,32,128]{2,1,0:T(8,128)(2,1)} reshape(bf16[4,32,4,32]{3,2,1,0:T(4,128)(2,1)} %param.8) | data formatting | bytes 65536 | tf_op jit(solution)/shard_map/reshape | solution.py:401
  1.7 74.7 %shard_map.64 = bf16[4,32,1024]{2,1,0:T(8,128)(2,1)} custom-call(s32[4]{0:T(128)} %pair_ref.1, s32[8]{0:T(128)} %used_ref.1, bf16[4,32,1024]{2,1,0:T(8,128)(2,1)} %amp.1, bf16[4,1024,1024]{2,1,0:T(8,128)(2,1)} %ints.1, bf16[4,32,128]{2,1,0:T(8,128)(2,1)} %reshape.3.hole, f32[4,32,1024]{2,1,0:T(8,128)} %den.1), custom_call_target="tpu_custom_call" | custom-call | tf_op jit(solution)/shard_map/pallas_call | solution.py:406
  76.4 1.7 %copy.8 = bf16[4,32,1024]{2,1,0:T(8,128)(2,1)} copy(bf16[4,32,1024]{2,1,0:T(8,128)(2,1)} %shard_map.64) | data formatting | bytes 524288
